TPU v7x, 32 devices: a whole 2x2x4 slice. The times are simulated.
32 devices in a mesh: groups: 2 (over y), space: 4 (over z), dp: 2 (over x), chan: 2 (over core).
Axes of the slice: x: 2, y: 2, z: 4, core: 2. Of those that a mesh axis runs over, the one named last changes fastest.
Arguments:
- grid: bfloat16 [4, 1024, 512], P(('groups', 'dp'), 'space'), parts along dimension 0, may hold values from -6 to 6
- mesh_nodes: bfloat16 [4, 512, 512], P(('groups', 'dp'), 'space'), parts along dimension 0, may hold values from -6 to 6
- cot: bfloat16 [4, 512, 512], P(('groups', 'dp'), 'space'), parts along dimension 0, may hold values from -6 to 6
- enc_send: bfloat16 [512, 512], P(None, 'chan'), may hold values from -0.25 to 0.25
- enc_recv: bfloat16 [512, 512], P(None, 'chan'), may hold values from -0.25 to 0.25
- enc_out: bfloat16 [512, 512], P('chan'), may hold values from -0.25 to 0.25
- proc_send: bfloat16 [512, 512], P(None, 'chan'), may hold values from -0.25 to 0.25
- proc_recv: bfloat16 [512, 512], P(None, 'chan'), may hold values from -0.25 to 0.25
- proc_out: bfloat16 [512, 512], P('chan'), may hold values from -0.25 to 0.25
- enc_sender: int32 [2048], P('space'), may hold values from 0 to 1023, as said below
- enc_receiver: int32 [2048], P('space'), may hold values from 0 to 511, as said below
- enc_count: int32 [4], P('space'), may hold values from 256 to 512, as said below
- proc_sender: int32 [2048], P('space'), may hold values from 0 to 511, as said below
- proc_receiver: int32 [2048], P('space'), may hold values from 0 to 511, as said below
- proc_count: int32 [4], P('space'), may hold values from 256 to 512, as said below
Outputs:
- mesh_out: bfloat16 [4, 512, 512], P(('groups', 'dp'), 'space'), parts along dimension 0
- grid_grad: float32 [4, 1024, 512], P(('groups', 'dp'), 'space'), parts along dimension 0
- mesh_grad: float32 [4, 512, 512], P(('groups', 'dp'), 'space'), parts along dimension 0
- enc_send_grad: float32 [1024, 512], P(('groups', 'space', 'dp'), 'chan'), parts along dimension 0
- enc_recv_grad: float32 [1024, 512], P(('groups', 'space', 'dp'), 'chan'), parts along dimension 0
- enc_out_grad: float32 [1024, 512], P(('groups', 'chan'), ('space', 'dp')), parts along dimension 0
- proc_send_grad: float32 [1024, 512], P(('groups', 'space', 'dp'), 'chan'), parts along dimension 0
- proc_recv_grad: float32 [1024, 512], P(('groups', 'space', 'dp'), 'chan'), parts along dimension 0
- proc_out_grad: float32 [1024, 512], P(('groups', 'chan'), ('space', 'dp')), parts along dimension 0
There are 2 independent parts, one for each index of `groups`. A program takes and returns all parts, laid end to end along the dimension named above; an argument that names none is the same for every part. Nothing has to cross between parts.
Inputs may be any that keep to these rules, and one draw needn't show every extreme that they name: `enc_sender`: grid nodes are numbered region by region, 256 to a region; block k holds slots k * 512 to (k + 1) * 512 - 1. In every block, padded slots included, at most 16 slots name senders of any one other region, and some other region supplies exactly 16. `enc_receiver`: mesh nodes are numbered region by region, 128 to a region; every slot of block k names a mesh node of region k. The first enc_count[k] slots of block k are live, the rest padding; some block is full. `proc_sender`: block k holds slots k * 512 to (k + 1) * 512 - 1. In every block, padded slots included, at most 16 slots name senders of any one other region, and some other region supplies exactly 16. `proc_receiver`: every slot of block k names a mesh node of region k. The first proc_count[k] slots of block k are live, the rest padding; some block is full.
All inputs are finite; a program needn't handle non-finite values.
Results may differ from a plain program's by a relative error of at most 0.0062.
Values may be sent and summed in bfloat16 or wider, within the bound.
A program may use at most 64 MiB of HBM per device.

v0:
```python
import jax
import jax.numpy as jnp
from jax import lax
from jax.sharding import PartitionSpec as P

CAP = 16


def times_transposed(left, right):
    return lax.dot_general(
        left, right, (((1,), (1,)), ((), ())), preferred_element_type=jnp.float32
    )


def left_transposed(left, right):
    return lax.dot_general(
        left, right, (((0,), (0,)), ((), ())), preferred_element_type=jnp.float32
    )


def exact_product(left, right):
    return jnp.dot(left, right, preferred_element_type=jnp.float32, precision=lax.Precision.HIGHEST)


def region_plan(sender, live_count, node_total, regions, own_region, slot_total):
    owners = sender // node_total
    local_row = sender - owners * node_total
    remote = owners != own_region
    edge_total = sender.shape[0]
    live_mask = (jnp.arange(edge_total) < live_count[0]).astype(jnp.float32)
    by_owner = ((owners[:, None] == jnp.arange(regions)[None, :]) & remote[:, None]).astype(
        jnp.int32
    )
    earlier = jnp.cumsum(by_owner, axis=0) - by_owner
    position = jnp.sum(earlier * by_owner, axis=1)
    slot_code = jnp.where(remote, owners * slot_total + position, regions * slot_total)
    requests = (
        jnp.zeros((regions * slot_total,), jnp.int32).at[slot_code].set(local_row + 1, mode="drop")
    )
    lookup = jnp.where(remote, node_total + slot_code, local_row)
    local_scatter = (
        (local_row[None, :] == jnp.arange(node_total)[:, None]) & jnp.logical_not(remote)[None, :]
    ).astype(jnp.float32)
    return (live_mask, slot_code, requests.reshape(regions, slot_total), lookup, local_scatter)


def receiver_scatter(receiver, own_region, node_total):
    local_row = receiver - own_region * node_total
    return (local_row, (local_row[None, :] == jnp.arange(node_total)[:, None]).astype(jnp.float32))


def fetch_rows(block, wanted):
    picked = jnp.take(block, jnp.maximum(wanted - 1, 0), axis=0)
    arrived = lax.all_to_all(picked, "space", split_axis=0, concat_axis=0, tiled=True)
    return jnp.concatenate([block, arrived.reshape(-1, block.shape[1])], axis=0)


def core_total(terms):
    return lax.psum(terms, "chan")


def edge_forward(sender_rows, receiver_rows, w_send, w_recv, w_out, live_mask):
    preact = jnp.dot(sender_rows, w_send, preferred_element_type=jnp.float32) + jnp.dot(
        receiver_rows, w_recv, preferred_element_type=jnp.float32
    )
    gate_value = jax.nn.sigmoid(preact)
    activation = (preact * gate_value).astype(jnp.bfloat16)
    message = jnp.dot(activation, w_out, preferred_element_type=jnp.float32) * live_mask[:, None]
    return (preact, gate_value, activation, message)


def edge_backward(message_grad, preact, gate_value, w_out):
    hidden_grad = times_transposed(message_grad, w_out)
    return (hidden_grad * gate_value * (1.0 + preact * (1.0 - gate_value))).astype(jnp.bfloat16)


def sender_terms(preact_grad, w_send, slot_code, wanted, local_scatter, regions, slot_total):
    input_grad = times_transposed(preact_grad, w_send)
    local_part = exact_product(local_scatter, input_grad)
    outgoing = (
        jnp.zeros((regions * slot_total, input_grad.shape[1]), jnp.float32)
        .at[slot_code]
        .set(input_grad, mode="drop")
    )
    incoming = (
        lax.all_to_all(
            outgoing.reshape(regions, slot_total, -1).astype(jnp.bfloat16),
            "space",
            split_axis=0,
            concat_axis=0,
            tiled=True,
        )
        .astype(jnp.float32)
        .reshape(regions * slot_total, -1)
    )
    node_total = local_scatter.shape[0]
    owner_scatter = (wanted.reshape(-1)[None, :] - 1 == jnp.arange(node_total)[:, None]).astype(
        jnp.float32
    )
    return local_part + exact_product(owner_scatter, incoming)


def body(
    grid,
    mesh_nodes,
    cot,
    enc_send,
    enc_recv,
    enc_out,
    proc_send,
    proc_recv,
    proc_out,
    enc_sender,
    enc_receiver,
    enc_count,
    proc_sender,
    proc_receiver,
    proc_count,
):
    regions = lax.axis_size("space")
    own_region = lax.axis_index("space")
    grid_block = grid[0]
    mesh_block = mesh_nodes[0]
    cot_block = cot[0]
    grid_total = grid_block.shape[0]
    mesh_total = mesh_block.shape[0]
    enc_plan = region_plan(enc_sender, enc_count, grid_total, regions, own_region, CAP)
    proc_plan = region_plan(proc_sender, proc_count, mesh_total, regions, own_region, CAP)
    enc_wanted, proc_wanted = (
        lax.all_to_all(enc_plan[2], "space", split_axis=0, concat_axis=0, tiled=True),
        lax.all_to_all(proc_plan[2], "space", split_axis=0, concat_axis=0, tiled=True),
    )
    enc_local_recv, enc_onehot = receiver_scatter(enc_receiver, own_region, mesh_total)
    proc_local_recv, proc_onehot = receiver_scatter(proc_receiver, own_region, mesh_total)
    enc_table = fetch_rows(grid_block, enc_wanted)
    enc_senders = jnp.take(enc_table, enc_plan[3], axis=0)
    enc_receivers = jnp.take(mesh_block, enc_local_recv, axis=0)
    enc_pre, enc_gate, enc_act, enc_msg = edge_forward(
        enc_senders, enc_receivers, enc_send, enc_recv, enc_out, enc_plan[0]
    )
    enc_summed = core_total(exact_product(enc_onehot, enc_msg))
    mesh_mid = (mesh_block.astype(jnp.float32) + enc_summed).astype(jnp.bfloat16)
    proc_table = fetch_rows(mesh_mid, proc_wanted)
    proc_senders = jnp.take(proc_table, proc_plan[3], axis=0)
    proc_receivers = jnp.take(mesh_mid, proc_local_recv, axis=0)
    proc_pre, proc_gate, proc_act, proc_msg = edge_forward(
        proc_senders, proc_receivers, proc_send, proc_recv, proc_out, proc_plan[0]
    )
    proc_summed = core_total(exact_product(proc_onehot, proc_msg))
    mesh_out = (mesh_mid.astype(jnp.float32) + proc_summed).astype(jnp.bfloat16)
    proc_dmsg = jnp.where(
        proc_plan[0][:, None] > 0,
        jnp.take(cot_block, proc_local_recv, axis=0),
        jnp.zeros((), jnp.bfloat16),
    )
    proc_dpre = edge_backward(proc_dmsg, proc_pre, proc_gate, proc_out)
    proc_out_grad = left_transposed(proc_act, proc_dmsg)
    proc_send_grad = left_transposed(proc_senders, proc_dpre)
    proc_recv_grad = left_transposed(proc_receivers, proc_dpre)
    mesh_part = exact_product(proc_onehot, times_transposed(proc_dpre, proc_recv)) + sender_terms(
        proc_dpre, proc_send, proc_plan[1], proc_wanted, proc_plan[4], regions, CAP
    )
    mesh_mid_grad = cot_block.astype(jnp.float32) + core_total(mesh_part)
    enc_dmsg = jnp.where(
        enc_plan[0][:, None] > 0,
        jnp.take(mesh_mid_grad.astype(jnp.bfloat16), enc_local_recv, axis=0),
        jnp.zeros((), jnp.bfloat16),
    )
    enc_dpre = edge_backward(enc_dmsg, enc_pre, enc_gate, enc_out)
    enc_out_grad = left_transposed(enc_act, enc_dmsg)
    enc_send_grad = left_transposed(enc_senders, enc_dpre)
    enc_recv_grad = left_transposed(enc_receivers, enc_dpre)
    grid_part = sender_terms(enc_dpre, enc_send, enc_plan[1], enc_wanted, enc_plan[4], regions, CAP)
    receiver_part = exact_product(enc_onehot, times_transposed(enc_dpre, enc_recv))
    grid_summed, receiver_summed = core_total((grid_part, receiver_part))
    mesh_grad = mesh_mid_grad + receiver_summed
    shared = (
        lax.psum_scatter(enc_send_grad, ("space", "dp"), scatter_dimension=0, tiled=True),
        lax.psum_scatter(enc_recv_grad, ("space", "dp"), scatter_dimension=0, tiled=True),
        lax.psum_scatter(enc_out_grad, ("space", "dp"), scatter_dimension=1, tiled=True),
        lax.psum_scatter(proc_send_grad, ("space", "dp"), scatter_dimension=0, tiled=True),
        lax.psum_scatter(proc_recv_grad, ("space", "dp"), scatter_dimension=0, tiled=True),
        lax.psum_scatter(proc_out_grad, ("space", "dp"), scatter_dimension=1, tiled=True),
    )
    return (
        mesh_out[None],
        grid_summed[None],
        mesh_grad[None],
        shared[0],
        shared[1],
        shared[2],
        shared[3],
        shared[4],
        shared[5],
    )


def solution(mesh):
    placed = (
        P(("groups", "dp"), "space", None),
        P(("groups", "dp"), "space", None),
        P(("groups", "dp"), "space", None),
        P(None, "chan"),
        P(None, "chan"),
        P("chan", None),
        P(None, "chan"),
        P(None, "chan"),
        P("chan", None),
        P("space"),
        P("space"),
        P("space"),
        P("space"),
        P("space"),
        P("space"),
    )
    return jax.shard_map(
        body,
        mesh=mesh,
        in_specs=placed,
        out_specs=(
            P(("groups", "dp"), "space", None),
            P(("groups", "dp"), "space", None),
            P(("groups", "dp"), "space", None),
            P(("groups", "space", "dp"), "chan"),
            P(("groups", "space", "dp"), "chan"),
            P(("groups", "chan"), ("space", "dp")),
            P(("groups", "space", "dp"), "chan"),
            P(("groups", "space", "dp"), "chan"),
            P(("groups", "chan"), ("space", "dp")),
        ),
        check_vma=False,
    )
```

profile of v0, /device:TPU:0, one launch (start us, length us, event | category | flops | bytes accessed | tf_op | source)
XLA Modules:
  0.0 566.8 jit_solution(7288959292029869117)
XLA Ops:
  8.5 1.2 reduce-window.14
  10.8 2.4 scatter_custom_fusion
  13.9 6.3 %all-to-all-start = ((s32[4,1,16]{2,1,0:T(1,128)}), s32[4,1,16]{2,1,0:T(1,128)S(1)}, u32[]{:S(2)}, u32[]{:S(2)}) async-start(s32[4,1,16]{2,1,0:T(1,128)} %bitcast.5), calls=%async_computation | async-start | bytes 4096 | tf_op jit(solution)/shard_map/all_to_all | solution.py:130
  20.8 1.2 reduce-window.16
  25.4 2.4 scatter_custom_fusion.1
  28.5 2.0 gather_fusion.6
  30.5 2.0 gather_fusion.4
  32.5 5.1 all-to-all-start.2
  37.6 5.4 all-to-all-done.2
  44.6 3.3 all-to-all-start.1
  48.6 5.1 all-to-all-done.1
  53.7 2.0 gather_fusion.1
  58.5 1.2 fusion.12
  59.9 16.9 %all-reduce.5.cloned.1.call-done = f32[128,512]{1,0:T(8,128)} async-done(((f32[128,512]{1,0:T(8,128)}), f32[128,512]{1,0:T(8,128)}) %all-reduce.5.cloned.1.call-update) | async-done | bytes 262160 | tf_op jit(solution)/shard_map/psum | solution.py:59
  76.8 1.0 add_convert_fusion.1
  79.2 4.9 all-to-all-start.3
  85.2 2.0 gather_fusion.5
  87.2 2.6 all-to-all-done.3
  89.8 2.0 gather_fusion.3
  95.7 2.4 scatter_custom_fusion.2
  99.9 3.3 all-to-all-start.4
  103.8 5.1 all-to-all-done.4
  111.2 1.2 fusion.10
  112.4 14.4 %all-reduce.7.cloned.1.call-done = f32[128,512]{1,0:T(8,128)} async-done(((f32[128,512]{1,0:T(8,128)}), f32[128,512]{1,0:T(8,128)}) %all-reduce.7.cloned.1.call-update) | async-done | bytes 262160 | tf_op jit(solution)/shard_map/psum | solution.py:59
  126.8 1.0 fusion.23
  127.8 2.0 gather_fusion.7
  132.9 2.4 scatter_custom_fusion.3
  135.9 4.9 all-to-all-start.5
  140.8 1.2 fusion.11
  142.0 4.5 all-to-all-done.5
  147.4 1.5 fusion
  150.0 1.2 fusion.19
  151.3 1.0 copy-done.5
  152.3 1.2 fusion.22
  153.6 1.0 copy-done.13
  154.6 1.4 fusion.70
  156.1 1.0 copy-done.15
  157.0 1.2 fusion.17
  158.4 1.3 fusion.21
  160.7 1.4 fusion.71
  162.1 5.2 all-reduce.9.cloned.1.call-done
  167.3 1.7 fusion.24
  169.8 64.8 %reduce-scatter.13.cloned.1.call-done = f32[64,256]{1,0:T(8,128)} async-done(((f32[512,256]{1,0:T(8,128)}), f32[64,256]{1,0:T(8,128)}) %reduce-scatter.13.cloned.1.call-update) | async-done | bytes 65552 | tf_op jit(solution)/shard_map/reduce_scatter | solution.py:181
  234.6 64.7 %reduce-scatter.15.cloned.1.call-done = f32[64,256]{1,0:T(8,128)} async-done(((f32[512,256]{1,0:T(8,128)}), f32[64,256]{1,0:T(8,128)}) %reduce-scatter.15.cloned.1.call-update) | async-done | bytes 65552 | tf_op jit(solution)/shard_map/reduce_scatter | solution.py:182
  299.3 65.1 %reduce-scatter.17.cloned.1.call-done = f32[256,64]{0,1:T(8,128)} async-done(((f32[256,512]{0,1:T(8,128)}), f32[256,64]{0,1:T(8,128)}) %reduce-scatter.17.cloned.1.call-update) | async-done | bytes 65552 | tf_op jit(solution)/shard_map/reduce_scatter | solution.py:183
  364.4 64.9 %reduce-scatter.7.cloned.1.call-done = f32[64,256]{1,0:T(8,128)} async-done(((f32[512,256]{1,0:T(8,128)}), f32[64,256]{1,0:T(8,128)}) %reduce-scatter.7.cloned.1.call-update) | async-done | bytes 65552 | tf_op jit(solution)/shard_map/reduce_scatter | solution.py:178
  429.3 65.3 %reduce-scatter.9.cloned.1.call-done = f32[64,256]{1,0:T(8,128)} async-done(((f32[512,256]{1,0:T(8,128)}), f32[64,256]{1,0:T(8,128)}) %reduce-scatter.9.cloned.1.call-update) | async-done | bytes 65552 | tf_op jit(solution)/shard_map/reduce_scatter | solution.py:179
  494.6 64.8 %reduce-scatter.11.cloned.1.call-done = f32[256,64]{0,1:T(8,128)} async-done(((f32[256,512]{0,1:T(8,128)}), f32[256,64]{0,1:T(8,128)}) %reduce-scatter.11.cloned.1.call-update) | async-done | bytes 65552 | tf_op jit(solution)/shard_map/reduce_scatter | solution.py:180
  (201 shorter events, 30.9 us)
Async XLA Ops:
  7.2 84.6 %copy-start = (bf16[512,256]{1,0:T(8,128)(2,1)S(1)}, bf16[512,256]{1,0:T(8,128)(2,1)}, u32[]{:S(2)}) copy-start(bf16[512,256]{1,0:T(8,128)(2,1)} %param.23) | copy-start | bytes 786436
  9.7 10.5 %copy-start.33 = (s32[512]{0:T(512)S(1)}, s32[512]{0:T(512)}, u32[]{:S(2)}) copy-start(s32[512]{0:T(512)} %param.29) | copy-start | bytes 6148
  9.9 18.6 %copy-start.1 = (bf16[1,128,512]{2,1,0:T(8,128)(2,1)S(1)}, bf16[1,128,512]{2,1,0:T(8,128)(2,1)}, u32[]{:S(2)}) copy-start(bf16[1,128,512]{2,1,0:T(8,128)(2,1)} %param.19) | copy-start | bytes 393220
  10.3 45.4 %copy-start.47 = (pred[512]{0:T(512)(128)(4,1)}, pred[512]{0:T(512)(128)(4,1)S(1)}, u32[]{:S(2)}) copy-start(pred[512]{0:T(512)(128)(4,1)S(1)} %get-tuple-element.30) | copy-start | bytes 1540
  13.9 18.6 %all-to-all-start = ((s32[4,1,16]{2,1,0:T(1,128)}), s32[4,1,16]{2,1,0:T(1,128)S(1)}, u32[]{:S(2)}, u32[]{:S(2)}) async-start(s32[4,1,16]{2,1,0:T(1,128)} %bitcast.5), calls=%async_computation | async-start | bytes 4096 | tf_op jit(solution)/shard_map/all_to_all | solution.py:130
  22.6 2.8 copy-start.40
  22.6 69.2 %copy-start.49 = (pred[512]{0:T(512)(128)(4,1)}, pred[512]{0:T(512)(128)(4,1)S(1)}, u32[]{:S(2)}) copy-start(pred[512]{0:T(512)(128)(4,1)S(1)} %get-tuple-element.25) | copy-start | bytes 1540
  24.6 31.9 %copy-start.42 = (pred[512]{0:T(512)(128)(4,1)}, pred[512]{0:T(512)(128)(4,1)S(1)}, u32[]{:S(2)}) copy-start(pred[512]{0:T(512)(128)(4,1)S(1)} %get-tuple-element.28) | copy-start | bytes 1540
  25.3 5.2 copy-start.30
  25.3 68.0 %copy-start.44 = (pred[512]{0:T(512)(128)(4,1)}, pred[512]{0:T(512)(128)(4,1)S(1)}, u32[]{:S(2)}) copy-start(pred[512]{0:T(512)(128)(4,1)S(1)} %get-tuple-element.23) | copy-start | bytes 1540
  28.5 2.0 copy-start.2
  30.5 62.8 %copy-start.12 = (bf16[512,512]{1,0:T(8,128)(2,1)}, bf16[512,512]{1,0:T(8,128)(2,1)S(1)}, u32[]{:S(2)}) copy-start(bf16[512,512]{1,0:T(8,128)(2,1)S(1)} %gather_fusion.6) | copy-start | bytes 1572868
  30.5 12.7 %copy-start.3 = (bf16[1,256,512]{2,1,0:T(8,128)(2,1)S(1)}, bf16[1,256,512]{2,1,0:T(8,128)(2,1)}, u32[]{:S(2)}) copy-start(bf16[1,256,512]{2,1,0:T(8,128)(2,1)} %param.17) | copy-start | bytes 786436
  32.5 10.6 %all-to-all-start.2 = ((s32[4,1,16]{2,1,0:T(1,128)}), s32[4,1,16]{2,1,0:T(1,128)S(1)}, u32[]{:S(2)}, u32[]{:S(2)}) async-start(s32[4,1,16]{2,1,0:T(1,128)} %bitcast.12), calls=%async_computation.2 | async-start | bytes 4096 | tf_op jit(solution)/shard_map/all_to_all | solution.py:131
  44.6 9.0 %all-to-all-start.1 = ((bf16[4,16,512]{2,1,0:T(8,128)(2,1)}), bf16[4,16,512]{2,1,0:T(8,128)(2,1)S(1)}, u32[]{:S(2)}, u32[]{:S(2)}) async-start(bf16[4,16,512]{2,1,0:T(8,128)(2,1)} %broadcast_select_fusion.13), calls=%async_computation.1 | async-start | bytes 131072 | tf_op jit(solution)/shard_map/all_to_all | solution.py:54
  47.9 28.8 %all-reduce.5.cloned.1.call-start = ((), (), s32[]{:S(2)}) async-start(), calls=%async_computation.12 | async-start | bytes 524288 | tf_op jit(solution)/shard_map/psum | solution.py:59
  53.7 2.0 copy-start.28
  55.7 1.1 copy-start.8
  79.2 10.6 %all-to-all-start.3 = ((bf16[4,16,512]{2,1,0:T(8,128)(2,1)}), bf16[4,16,512]{2,1,0:T(8,128)(2,1)S(1)}, u32[]{:S(2)}, u32[]{:S(2)}) async-start(bf16[4,16,512]{2,1,0:T(8,128)(2,1)} %broadcast_select_fusion.12), calls=%async_computation.3 | async-start | bytes 131072 | tf_op jit(solution)/shard_map/all_to_all | solution.py:54
  84.0 9.3 %copy-start.56 = (pred[512]{0:T(512)(128)(4,1)}, pred[512]{0:T(512)(128)(4,1)S(1)}, u32[]{:S(2)}) copy-start(pred[512]{0:T(512)(128)(4,1)S(1)} %broadcast_compare_fusion) | copy-start | bytes 1540
  87.2 5.4 copy-start.4
  91.8 1.1 copy-start.7
  99.9 9.0 %all-to-all-start.4 = ((bf16[4,16,512]{2,1,0:T(8,128)(2,1)}), bf16[4,16,512]{2,1,0:T(8,128)(2,1)S(1)}, u32[]{:S(2)}, u32[]{:S(2)}) async-start(bf16[4,16,512]{2,1,0:T(8,128)(2,1)} %bitcast.18), calls=%async_computation.4 | async-start | bytes 131072 | tf_op jit(solution)/shard_map/all_to_all | solution.py:86
  103.2 23.5 %all-reduce.7.cloned.1.call-start = ((), (), s32[]{:S(2)}) async-start(), calls=%async_computation.13 | async-start | bytes 524288 | tf_op jit(solution)/shard_map/psum | solution.py:59
  103.8 5.1 copy-start.34
  112.4 15.4 %copy-start.31 = (s32[1024]{0:T(1024)S(1)}, s32[1024]{0:T(1024)}, u32[]{:S(2)}) copy-start(s32[1024]{0:T(1024)} %copy-done.30) | copy-start | bytes 12292
  127.8 2.8 copy-start.22
  127.8 2.8 copy-start.43
  127.8 2.8 copy-start.54
  127.8 2.8 copy-start.55
  135.9 10.6 %all-to-all-start.5 = ((bf16[4,16,512]{2,1,0:T(8,128)(2,1)}), bf16[4,16,512]{2,1,0:T(8,128)(2,1)S(1)}, u32[]{:S(2)}, u32[]{:S(2)}) async-start(bf16[4,16,512]{2,1,0:T(8,128)(2,1)} %bitcast.114), calls=%async_computation.5 | async-start | bytes 131072 | tf_op jit(solution)/shard_map/all_to_all | solution.py:86
  140.8 26.5 %all-reduce.9.cloned.1.call-start = ((), (), s32[]{:S(2)}) async-start(), calls=%async_computation.20 | async-start | bytes 2097152 | tf_op jit(solution)/shard_map/psum | solution.py:59
  142.0 4.5 copy-start.41
  148.9 1.1 copy-start.19
  148.9 1.1 copy-start.50
  148.9 85.7 %reduce-scatter.13.cloned.1.call-start = ((), (), s32[]{:S(2)}) async-start(), calls=%async_computation.17 | async-start | bytes 589824 | tf_op jit(solution)/shard_map/reduce_scatter | solution.py:181
  151.3 148.0 %reduce-scatter.15.cloned.1.call-start = ((), (), s32[]{:S(2)}) async-start(), calls=%async_computation.18 | async-start | bytes 589824 | tf_op jit(solution)/shard_map/reduce_scatter | solution.py:182
  152.3 1.3 copy-start.26
  153.5 1.0 copy-start.13
  153.5 1.0 copy-start.57
  153.6 210.9 %reduce-scatter.17.cloned.1.call-start = ((), (), s32[]{:S(2)}) async-start(), calls=%async_computation.19 | async-start | bytes 589824 | tf_op jit(solution)/shard_map/reduce_scatter | solution.py:183
  156.0 273.3 %reduce-scatter.7.cloned.1.call-start = ((), (), s32[]{:S(2)}) async-start(), calls=%async_computation.14 | async-start | bytes 589824 | tf_op jit(solution)/shard_map/reduce_scatter | solution.py:178
  158.3 336.3 %reduce-scatter.9.cloned.1.call-start = ((), (), s32[]{:S(2)}) async-start(), calls=%async_computation.15 | async-start | bytes 589824 | tf_op jit(solution)/shard_map/reduce_scatter | solution.py:179
  158.3 1.3 copy-start.23
  159.6 399.8 %reduce-scatter.11.cloned.1.call-start = ((), (), s32[]{:S(2)}) async-start(), calls=%async_computation.16 | async-start | bytes 589824 | tf_op jit(solution)/shard_map/reduce_scatter | solution.py:180
  167.3 1.7 copy-start.6
  167.3 1.7 copy-start.27
  169.0 390.4 %copy-start.20 = (f32[1,256,512]{2,1,0:T(8,128)S(1)}, f32[1,256,512]{2,1,0:T(8,128)}, u32[]{:S(2)}) copy-start(f32[1,256,512]{2,1,0:T(8,128)} %get-tuple-element.36) | copy-start | bytes 1572868
  (25 other events, 21.7 us)
Sparse Core Ops, SparseCore 0:
  59.9 16.8 all-reduce.4
  110.0 16.7 all-reduce.6
  149.1 18.2 all-reduce.8
  171.4 63.1 reduce-scatter.12
  238.4 60.9 reduce-scatter.14
  303.5 60.9 reduce-scatter.16
  368.3 60.9 reduce-scatter.6
  433.6 60.9 reduce-scatter.8
  498.6 60.8 reduce-scatter.10
where the time goes:
time: 568 us; the launch traced here: 567 us
  waiting for transfers between devices  449 us (79%)
  local copies, waits for them, and re-layouts  41.9 us (7%)
  starting transfers between devices  28 us (5%)
  matrix products  19.2 us (3%)
  between operations  15.9 us (3%)
  other arithmetic  12.7 us (2%)
    reduce_scatter x1, waiting for transfers between devices, body(): lax.psum_scatter(enc_recv_grad, ('space', 'dp'), scatter_dimension=0, til...  65.3 us
    reduce_scatter x1, waiting for transfers between devices, body(): lax.psum_scatter(proc_out_grad, ('space', 'dp'), scatter_dimension=1, til...  65.1 us
    reduce_scatter x1, waiting for transfers between devices, body(): lax.psum_scatter(enc_send_grad, ('space', 'dp'), scatter_dimension=0, til...  64.9 us
    reduce_scatter x1, waiting for transfers between devices, body(): lax.psum_scatter(proc_send_grad, ('space', 'dp'), scatter_dimension=0, ti...  64.8 us
    reduce_scatter x1, waiting for transfers between devices, body(): lax.psum_scatter(enc_out_grad, ('space', 'dp'), scatter_dimension=1, tile...  64.8 us
    reduce_scatter x1, waiting for transfers between devices, body(): lax.psum_scatter(proc_recv_grad, ('space', 'dp'), scatter_dimension=0, ti...  64.7 us
    psum x3, waiting for transfers between devices, core_total(): return lax.psum(terms, 'chan')  36.5 us
    unnamed x119, local copies, waits for them, and re-layouts  15.9 us
  transfers between devices with their start and end apart: 15, of which 14 were waited for; matrix products, arithmetic and copies ran while one was open for 5% of the time, Pallas kernels for 0%

commit v1 on v0

--- a/solution.py
+++ b/solution.py
@@ -1,6 +1,10 @@
+import functools
+
 import jax
 import jax.numpy as jnp
 from jax import lax
+from jax.experimental import pallas as pl
+from jax.experimental.pallas import tpu as pltpu
 from jax.sharding import PartitionSpec as P
 
 CAP = 16
@@ -195,6 +199,470 @@
     )
 
 
+F32 = jnp.float32
+BF16 = jnp.bfloat16
+
+
+def dot(left, right):
+    return jnp.dot(left, right, preferred_element_type=F32)
+
+
+def halves(values):
+    high = values.astype(BF16)
+    return high, (values - high.astype(F32)).astype(BF16)
+
+
+def dot_split(left, values):
+    high, low = halves(values)
+    return dot(left, high) + dot(left, low)
+
+
+def split_dot_transposed(values, right):
+    high, low = halves(values)
+    return times_transposed(high, right) + times_transposed(low, right)
+
+
+def split_dot(values, right):
+    high, low = halves(values)
+    return dot(high, right) + dot(low, right)
+
+
+def onehot(condition):
+    return jnp.where(condition, 1.0, 0.0).astype(BF16)
+
+
+def iota(shape, dim):
+    return lax.broadcasted_iota(jnp.int32, shape, dim).astype(F32)
+
+
+def fused_kernel(
+    regions,
+    samples,
+    cores,
+    grid_ref,
+    mesh_ref,
+    cot_ref,
+    enc_send,
+    enc_recv,
+    enc_out,
+    proc_send,
+    proc_recv,
+    proc_out,
+    enc_sender,
+    enc_receiver,
+    enc_count,
+    proc_sender,
+    proc_receiver,
+    proc_count,
+    mesh_out,
+    grid_grad,
+    mesh_grad,
+    g_enc_send,
+    g_enc_recv,
+    g_enc_out,
+    g_proc_send,
+    g_proc_recv,
+    g_proc_out,
+    req_out,
+    req_in,
+    row_out,
+    row_in,
+    term_out,
+    term_in,
+    part_out,
+    part_in,
+    last_out,
+    last_in,
+    full_grad,
+    pair_out,
+    pair_in,
+    ring_own,
+    ring_out,
+    ring_in,
+    send_sem,
+    recv_sem,
+):
+    own = lax.axis_index("space")
+    sample = lax.axis_index("dp")
+    core = lax.axis_index("chan")
+    edges = enc_sender.shape[1]
+    grid_total = grid_ref.shape[0]
+    mesh_total = mesh_ref.shape[0]
+    slots = regions * CAP
+    used = [0]
+
+    def space_at(step):
+        return lax.rem(own + step, regions)
+
+    def core_at(step):
+        return lax.rem(core + step, cores)
+
+    def place(s, d, c):
+        return {"space": s, "dp": d, "chan": c}
+
+    def send(src, dst, target):
+        index = used[0]
+        used[0] += 1
+        copy = pltpu.make_async_remote_copy(
+            src_ref=src,
+            dst_ref=dst,
+            send_sem=send_sem.at[index],
+            recv_sem=recv_sem.at[index],
+            device_id=target,
+            device_id_type=pl.DeviceIdType.MESH,
+        )
+        copy.start()
+        return copy
+
+    def arrive(copies):
+        for copy in copies:
+            copy.wait_recv()
+
+    everything = []
+    friends = []
+    for c_step in range(cores):
+        for s_step in range(regions):
+            if c_step or s_step:
+                friends.append(place(space_at(s_step), sample, core_at(c_step)))
+    for d_step in range(1, samples):
+        friends.append(place(own, lax.rem(sample + d_step, samples), core))
+    barrier = pltpu.get_barrier_semaphore()
+    for friend in friends:
+        pl.semaphore_signal(
+            barrier, inc=1, device_id=friend, device_id_type=pl.DeviceIdType.MESH
+        )
+
+    owner_rows = 16
+    before = onehot(iota((edges, edges), 0) < iota((edges, edges), 1))
+    owner_id = iota((owner_rows, edges), 0)
+    own_id = own.astype(F32)
+
+    def rows_of(sender_ref, receiver_ref, count_ref, total):
+        sender = sender_ref[...].astype(F32)
+        low = owner_id * total
+        owned = (sender >= low) & (sender < low + total)
+        local = (sender >= own_id * total) & (sender < own_id * total + total)
+        by_owner = jnp.where(owned & (owner_id != own_id), 1.0, 0.0)
+        earlier = dot(by_owner.astype(BF16), before)
+        code = jnp.sum(by_owner * (owner_id * CAP + earlier), axis=0, keepdims=True)
+        owner = jnp.sum(by_owner * owner_id, axis=0, keepdims=True)
+        code = jnp.where(local, -1.0, code)
+        local_row = jnp.where(local, sender - own_id * total, -1.0)
+        wanted = sender - owner * total + 1.0
+        receiver = receiver_ref[...].astype(F32) - own_id * mesh_total
+        alive = iota((1, edges), 1) < count_ref[...].astype(F32)
+        live_receiver = jnp.where(alive, receiver, -1.0)
+        match = code == iota((slots, edges), 0)
+        request = jnp.sum(jnp.where(match, wanted, 0.0), axis=1, keepdims=True)
+        return (local_row, code, receiver, live_receiver), onehot(match), request
+
+    enc_rows, enc_match, enc_request = rows_of(enc_sender, enc_receiver, enc_count, grid_total)
+    proc_rows, proc_match, proc_request = rows_of(
+        proc_sender, proc_receiver, proc_count, mesh_total
+    )
+    req_out[:, 0:CAP, :] = jnp.broadcast_to(enc_request, (slots, 128)).reshape(regions, CAP, 128)
+    req_out[:, CAP : 2 * CAP, :] = jnp.broadcast_to(proc_request, (slots, 128)).reshape(
+        regions, CAP, 128
+    )
+    req_in[own] = jnp.zeros(req_in.shape[1:], F32)
+    for graph in range(2):
+        row_in[graph, own] = jnp.zeros(row_in.shape[2:], BF16)
+        for c_step in range(cores):
+            term_in[graph, c_step, own] = jnp.zeros(term_in.shape[3:], BF16)
+
+    pl.semaphore_wait(barrier, len(friends))
+    requests = [
+        send(req_out.at[space_at(step)], req_in.at[own], place(space_at(step), sample, core))
+        for step in range(1, regions)
+    ]
+    everything += requests
+
+    columns = jnp.transpose(jnp.concatenate(list(enc_rows) + list(proc_rows), axis=0))
+
+    def tables(rows, first, total):
+        by_edge = [columns[:, first + i : first + i + 1] for i in range(4)]
+        return (
+            onehot(by_edge[0] == iota((edges, total), 1)),
+            onehot(by_edge[1] == iota((edges, slots), 1)),
+            onehot(by_edge[2] == iota((edges, mesh_total), 1)),
+            onehot(by_edge[3] == iota((edges, mesh_total), 1)),
+            onehot(rows[0] == iota((total, edges), 0)),
+            onehot(rows[2] == iota((mesh_total, edges), 0)),
+            onehot(rows[3] == iota((mesh_total, edges), 0)),
+        )
+
+    e_pick, e_far, e_recv, e_live, e_pick_t, e_recv_t, e_live_t = tables(
+        enc_rows, 0, grid_total
+    )
+    p_pick, p_far, p_recv, p_live, p_pick_t, p_recv_t, p_live_t = tables(
+        proc_rows, 4, mesh_total
+    )
+    grid_block = grid_ref[...]
+    mesh_block = mesh_ref[...]
+    cot_block = cot_ref[...]
+    enc_pre = dot_split(e_pick, dot(grid_block, enc_send[...])) + dot_split(
+        e_recv, dot(mesh_block, enc_recv[...])
+    )
+    proc_hidden = dot_split(p_live, times_transposed(cot_block, proc_out[...]))
+
+    def picks(graph, total):
+        asked = req_in[:, graph * CAP : (graph + 1) * CAP, :].reshape(slots, 128)
+        return onehot(asked[:, 0:1] == iota((slots, total), 1) + 1.0)
+
+    def send_rows(graph, pick, block):
+        row_out[graph] = dot(pick, block).astype(BF16).reshape(regions, CAP, -1)
+        return [
+            send(
+                row_out.at[graph, space_at(step)],
+                row_in.at[graph, own],
+                place(space_at(step), sample, core),
+            )
+            for step in range(1, regions)
+        ]
+
+    def far_rows(graph):
+        return row_in[graph].reshape(slots, -1)
+
+    arrive(requests)
+    enc_asked = picks(0, grid_total)
+    rows_sent = send_rows(0, enc_asked, grid_block)
+    everything += rows_sent
+    proc_asked = picks(1, mesh_total)
+    arrive(rows_sent)
+
+    enc_pre = enc_pre + dot_split(e_far, dot(far_rows(0), enc_send[...]))
+    enc_gate = jax.nn.sigmoid(enc_pre)
+    enc_act_sum = dot(e_live_t, (enc_pre * enc_gate).astype(BF16))
+    enc_sum = split_dot(enc_act_sum, enc_out[...])
+    other = place(own, sample, core_at(1))
+    part_out[0] = enc_sum
+    swapped = send(part_out.at[0], part_in.at[0], other)
+    everything.append(swapped)
+    enc_slope = enc_gate * (1.0 + enc_pre * (1.0 - enc_gate))
+    swapped.wait_recv()
+    mesh_mid = (mesh_block.astype(F32) + (part_out[0] + part_in[0])).astype(BF16)
+
+    rows_sent = send_rows(1, proc_asked, mesh_mid)
+    everything += rows_sent
+    proc_pre = dot_split(p_pick, dot(mesh_mid, proc_send[...])) + dot_split(
+        p_recv, dot(mesh_mid, proc_recv[...])
+    )
+    arrive(rows_sent)
+    proc_pre = proc_pre + dot_split(p_far, dot(far_rows(1), proc_send[...]))
+    proc_gate = jax.nn.sigmoid(proc_pre)
+    proc_dpre = (proc_hidden * (proc_gate * (1.0 + proc_pre * (1.0 - proc_gate)))).astype(BF16)
+
+    def send_terms(graph, match, dpre, weights):
+        far = dot(match, dpre).astype(BF16)
+        term_out[graph] = times_transposed(far, weights).astype(BF16).reshape(regions, CAP, -1)
+        copies = []
+        for step in range(1, regions):
+            for c_step in range(cores):
+                copies.append(
+                    send(
+                        term_out.at[graph, space_at(step)],
+                        term_in.at[graph, core, own],
+                        place(space_at(step), sample, core_at(c_step)),
+                    )
+                )
+        return far, copies
+
+    def returned(graph, asked):
+        return left_transposed(
+            jnp.concatenate([asked] * cores, axis=0),
+            term_in[graph].reshape(cores * slots, -1),
+        )
+
+    proc_far, terms = send_terms(1, proc_match, proc_dpre, proc_send[...])
+    everything += terms
+    proc_by_sender = dot(p_pick_t, proc_dpre)
+    proc_by_receiver = dot(p_recv_t, proc_dpre)
+    part_out[1] = split_dot_transposed(proc_by_receiver, proc_recv[...]) + split_dot_transposed(
+        proc_by_sender, proc_send[...]
+    )
+    swapped = send(part_out.at[1], part_in.at[1], other)
+    everything.append(swapped)
+
+    shard = full_grad.shape[3]
+
+    def share(index, gradient):
+        for s in range(regions):
+            for d in range(samples):
+                piece = gradient[(s * samples + d) * shard : (s * samples + d + 1) * shard]
+                full_grad[index, d, s] = piece
+                pair_out[index, d, s] = piece.astype(BF16)
+        copies = []
+        for step in range(1, samples):
+            target = lax.rem(sample + step, samples)
+            copies.append(
+                send(
+                    pair_out.at[index, target],
+                    pair_in.at[index, step - 1],
+                    place(own, target, core),
+                )
+            )
+        return copies
+
+    def pass_on(index, copies):
+        arrive(copies)
+        total = full_grad[index, sample]
+        for step in range(1, samples):
+            total = total + pair_in[index, step - 1].astype(F32)
+        ring_own[index] = total
+        ring_out[index] = total.astype(BF16)
+        return [
+            send(
+                ring_out.at[index, space_at(step)],
+                ring_in.at[index, step - 1],
+                place(space_at(step), sample, core),
+            )
+            for step in range(1, regions)
+        ]
+
+    def finish(index, copies):
+        arrive(copies)
+        total = ring_own[index, own]
+        for step in range(1, regions):
+            total = total + ring_in[index, step - 1].astype(F32)
+        return total
+
+    proc_act_sum = dot(p_live_t, (proc_pre * proc_gate).astype(BF16))
+    shared = {}
+    shared[5] = share(5, left_transposed(cot_block, proc_act_sum.astype(BF16)))
+    shared[3] = share(
+        3,
+        left_transposed(mesh_mid, proc_by_sender.astype(BF16))
+        + left_transposed(far_rows(1), proc_far),
+    )
+    shared[4] = share(4, left_transposed(mesh_mid, proc_by_receiver.astype(BF16)))
+    part_out[2] = split_dot(proc_act_sum, proc_out[...])
+    out_swap = send(part_out.at[2], part_in.at[2], other)
+    for index in (5, 3, 4):
+        everything += shared[index]
+    everything.append(out_swap)
+
+    arrive(terms)
+    swapped.wait_recv()
+    mesh_mid_grad = cot_block.astype(F32) + (
+        (part_out[1] + part_in[1]) + returned(1, proc_asked)
+    )
+
+    mid_rounded = mesh_mid_grad.astype(BF16)
+    enc_hidden = dot_split(e_live, times_transposed(mid_rounded, enc_out[...]))
+    enc_dpre = (enc_hidden * enc_slope).astype(BF16)
+    shared[2] = share(2, left_transposed(mid_rounded, enc_act_sum.astype(BF16)))
+    enc_by_sender = dot(e_pick_t, enc_dpre)
+    enc_by_receiver = dot(e_recv_t, enc_dpre)
+    enc_far, terms = send_terms(0, enc_match, enc_dpre, enc_send[...])
+    shared[0] = share(
+        0,
+        left_transposed(grid_block, enc_by_sender.astype(BF16))
+        + left_transposed(far_rows(0), enc_far),
+    )
+    shared[1] = share(1, left_transposed(mesh_block, enc_by_receiver.astype(BF16)))
+    last_out[0:grid_total] = split_dot_transposed(enc_by_sender, enc_send[...])
+    last_out[grid_total : grid_total + mesh_total] = split_dot_transposed(
+        enc_by_receiver, enc_recv[...]
+    )
+    last_swap = send(last_out, last_in, other)
+    everything += terms
+    for index in (2, 0, 1):
+        everything += shared[index]
+    everything.append(last_swap)
+
+    passed = {}
+    for index in (5, 3, 4, 2, 0, 1):
+        passed[index] = pass_on(index, shared[index])
+        everything += passed[index]
+
+    out_swap.wait_recv()
+    mesh_out[...] = (mesh_mid.astype(F32) + (part_out[2] + part_in[2])).astype(BF16)
+    arrive(terms)
+    last_swap.wait_recv()
+    grid_grad[...] = (last_out[0:grid_total] + last_in[0:grid_total]) + returned(0, enc_asked)
+    tail = slice(grid_total, grid_total + mesh_total)
+    mesh_grad[...] = mesh_mid_grad + (last_out[tail] + last_in[tail])
+
+    g_proc_out[...] = jnp.transpose(finish(5, passed[5]))
+    g_proc_send[...] = finish(3, passed[3])
+    g_proc_recv[...] = finish(4, passed[4])
+    g_enc_out[...] = jnp.transpose(finish(2, passed[2]))
+    g_enc_send[...] = finish(0, passed[0])
+    g_enc_recv[...] = finish(1, passed[1])
+    for copy in everything:
+        copy.wait_send()
+
+
+def fused_body(regions, samples, cores, grid, mesh_nodes, cot, *rest):
+    weights, indices = rest[:6], rest[6:]
+    grid_total, width = grid.shape[1:]
+    mesh_total = mesh_nodes.shape[1]
+    hidden = weights[0].shape[1]
+    shard = width // (regions * samples)
+    last_total = grid_total + mesh_total
+    copies = (regions - 1) * (3 + 2 * cores + 6) + 6 * (samples - 1) + 4
+    vmem = pl.BlockSpec(memory_space=pltpu.VMEM)
+    outs = pl.pallas_call(
+        functools.partial(fused_kernel, regions, samples, cores),
+        out_shape=(
+            jax.ShapeDtypeStruct((mesh_total, width), BF16),
+            jax.ShapeDtypeStruct((grid_total, width), F32),
+            jax.ShapeDtypeStruct((mesh_total, width), F32),
+            jax.ShapeDtypeStruct((shard, hidden), F32),
+            jax.ShapeDtypeStruct((shard, hidden), F32),
+            jax.ShapeDtypeStruct((hidden, shard), F32),
+            jax.ShapeDtypeStruct((shard, hidden), F32),
+            jax.ShapeDtypeStruct((shard, hidden), F32),
+            jax.ShapeDtypeStruct((hidden, shard), F32),
+        ),
+        in_specs=[vmem] * 15,
+        out_specs=(vmem,) * 9,
+        scratch_shapes=[
+            pltpu.VMEM((regions, 2 * CAP, 128), F32),
+            pltpu.VMEM((regions, 2 * CAP, 128), F32),
+            pltpu.VMEM((2, regions, CAP, width), BF16),
+            pltpu.VMEM((2, regions, CAP, width), BF16),
+            pltpu.VMEM((2, regions, CAP, width), BF16),
+            pltpu.VMEM((2, cores, regions, CAP, width), BF16),
+            pltpu.VMEM((3, mesh_total, width), F32),
+            pltpu.VMEM((3, mesh_total, width), F32),
+            pltpu.VMEM((last_total, width), F32),
+            pltpu.VMEM((last_total, width), F32),
+            pltpu.VMEM((6, samples, regions, shard, hidden), F32),
+            pltpu.VMEM((6, samples, regions, shard, hidden), BF16),
+            pltpu.VMEM((6, samples - 1, regions, shard, hidden), BF16),
+            pltpu.VMEM((6, regions, shard, hidden), F32),
+            pltpu.VMEM((6, regions, shard, hidden), BF16),
+            pltpu.VMEM((6, regions - 1, shard, hidden), BF16),
+            pltpu.SemaphoreType.DMA((copies,)),
+            pltpu.SemaphoreType.DMA((copies,)),
+        ],
+        compiler_params=pltpu.CompilerParams(
+            collective_id=0, has_side_effects=True, vmem_limit_bytes=48 * 2**20
+        ),
+    )(
+        grid[0],
+        mesh_nodes[0],
+        cot[0],
+        *weights,
+        *[index.reshape(1, -1) for index in indices],
+    )
+    return (outs[0][None], outs[1][None], outs[2][None], *outs[3:])
+
+
+def chosen_body(mesh):
+    regions, samples, cores = (mesh.shape[name] for name in ("space", "dp", "chan"))
+    shards = regions * samples
+
+    def run(*args):
+        width = args[0].shape[2]
+        if regions > 16 or samples < 2 or cores != 2 or width % (16 * shards):
+            return body(*args)
+        return fused_body(regions, samples, cores, *args)
+
+    return run
+
+
 def solution(mesh):
     placed = (
         P(("groups", "dp"), "space", None),
@@ -214,7 +682,7 @@
         P("space"),
     )
     return jax.shard_map(
-        body,
+        chosen_body(mesh),
         mesh=mesh,
         in_specs=placed,
         out_specs=(

time: 568 us -> 65.2 us (0.11)
  waiting for transfers between devices: 449 us -> 0 us
  Pallas kernels: 0 us -> 47.5 us
  starting transfers between devices: 28 us -> 0 us
  local copies, waits for them, and re-layouts: 41.9 us -> 15.2 us
  matrix products: 19.2 us -> 0 us
  between operations: 15.9 us -> 1.99 us
  other arithmetic: 12.7 us -> 0 us
    reduce_scatter x6 -> x0, waiting for transfers between devices: 390 us -> none  [the longest x1 65.3 us: body(): lax.psum_scatter(enc_recv_grad, ('space', 'dp'), scatter_dimension=0, til...]
    pallas_call x0 -> x1, Pallas kernels: none -> 47.5 us  [fused_body(): pl.pallas_call(functools.partial(fused_kernel, regions, samples, cores),...]
    psum x3 -> x0, waiting for transfers between devices: 36.5 us -> none  [core_total(): return lax.psum(terms, 'chan')]
    all_to_all x6 -> x0, starting transfers between devices: 27.7 us -> none  [the longest x2 8.14 us: fetch_rows(): lax.all_to_all(picked, 'space', split_axis=0, concat_axis=0, tiled=True)]
    all_to_all x6 -> x0, waiting for transfers between devices: 22.7 us -> none  [the longest x2 9.66 us: sender_terms(): lax.all_to_all(outgoing.reshape(regions, slot_total, -1).astype(jnp.bfloa...]
    dot_general x26 -> x0, matrix products: 19.2 us -> none  [the longest x6 7.78 us: left_transposed(): lax.dot_general(left, right, (((0,), (0,)), ((), ())), preferred_element_...]
    gather x8 -> x0, local copies, waits for them, and re-layouts: 13.2 us -> none  [the longest x1 1.97 us: body(): enc_receivers = jnp.take(mesh_block, enc_local_recv, axis=0)]
    scatter x4 -> x0, local copies, waits for them, and re-layouts: 9.68 us -> none  [the longest x2 4.87 us: region_plan(): jnp.zeros((regions * slot_total,), jnp.int32).at[slot_code]]
  transfers between devices with their start and end apart: 15 -> 0, of which waited for: 14 -> 0; matrix products, arithmetic and copies ran while one was open for 5% -> 0% of each run, Pallas kernels for 0% -> 0%
where the time goes in v1:
time: 65.2 us; the launch traced here: 64.7 us
  Pallas kernels  47.5 us (73%)
  local copies, waits for them, and re-layouts  15.2 us (23%)
  between operations  1.99 us (3%)
    pallas_call x1, Pallas kernels, fused_body(): pl.pallas_call(functools.partial(fused_kernel, regions, samples, cores),...  47.5 us
    unnamed x35, local copies, waits for them, and re-layouts  15.2 us

profile of v1, /device:TPU:0, one launch (start us, length us, event | category | flops | bytes accessed | tf_op | source)
XLA Modules:
  0.0 64.7 jit_solution(2008416848215358035)
XLA Ops:
  1.9 0.0 copy-start.12
  1.9 0.0 copy-start.11
  2.0 0.0 copy-start.10
  2.0 0.0 copy-start.9
  2.0 0.6 copy-done.12
  2.6 0.0 copy-done.11
  2.6 0.0 copy-done.10
  2.7 0.0 copy-done.9
  2.7 0.0 copy-start
  2.7 0.9 %copy-done = bf16[1,256,512]{2,1,0:T(8,128)(2,1)S(1)} copy-done((bf16[1,256,512]{2,1,0:T(8,128)(2,1)S(1)}, bf16[1,256,512]{2,1,0:T(8,128)(2,1)}, u32[]{:S(2)}) %copy-start) | copy-done | bytes 262168
  3.6 0.0 copy-start.1
  3.6 0.9 %copy-done.1 = bf16[512,256]{1,0:T(8,128)(2,1)S(1)} copy-done((bf16[512,256]{1,0:T(8,128)(2,1)S(1)}, bf16[512,256]{1,0:T(8,128)(2,1)}, u32[]{:S(2)}) %copy-start.1) | copy-done | bytes 262168
  4.6 0.0 copy-start.2
  4.6 0.9 %copy-done.2 = bf16[512,256]{1,0:T(8,128)(2,1)S(1)} copy-done((bf16[512,256]{1,0:T(8,128)(2,1)S(1)}, bf16[512,256]{1,0:T(8,128)(2,1)}, u32[]{:S(2)}) %copy-start.2) | copy-done | bytes 262168
  5.5 0.0 copy-start.3
  5.5 0.9 %copy-done.3 = bf16[256,512]{1,0:T(8,128)(2,1)S(1)} copy-done((bf16[256,512]{1,0:T(8,128)(2,1)S(1)}, bf16[256,512]{1,0:T(8,128)(2,1)}, u32[]{:S(2)}) %copy-start.3) | copy-done | bytes 262168
  6.5 0.0 copy-start.4
  6.5 0.9 %copy-done.4 = bf16[512,256]{1,0:T(8,128)(2,1)S(1)} copy-done((bf16[512,256]{1,0:T(8,128)(2,1)S(1)}, bf16[512,256]{1,0:T(8,128)(2,1)}, u32[]{:S(2)}) %copy-start.4) | copy-done | bytes 262168
  7.4 0.0 copy-start.5
  7.4 0.9 %copy-done.5 = bf16[512,256]{1,0:T(8,128)(2,1)S(1)} copy-done((bf16[512,256]{1,0:T(8,128)(2,1)S(1)}, bf16[512,256]{1,0:T(8,128)(2,1)}, u32[]{:S(2)}) %copy-start.5) | copy-done | bytes 262168
  8.4 0.0 copy-start.6
  8.4 0.9 %copy-done.6 = bf16[256,512]{1,0:T(8,128)(2,1)S(1)} copy-done((bf16[256,512]{1,0:T(8,128)(2,1)S(1)}, bf16[256,512]{1,0:T(8,128)(2,1)}, u32[]{:S(2)}) %copy-start.6) | copy-done | bytes 262168
  9.3 0.0 copy-start.7
  9.3 0.9 %copy-done.7 = bf16[1,128,512]{2,1,0:T(8,128)(2,1)S(1)} copy-done((bf16[1,128,512]{2,1,0:T(8,128)(2,1)S(1)}, bf16[1,128,512]{2,1,0:T(8,128)(2,1)}, u32[]{:S(2)}) %copy-start.7) | copy-done | bytes 131096
  10.2 0.0 copy-start.8
  10.2 0.9 %copy-done.8 = bf16[1,128,512]{2,1,0:T(8,128)(2,1)S(1)} copy-done((bf16[1,128,512]{2,1,0:T(8,128)(2,1)S(1)}, bf16[1,128,512]{2,1,0:T(8,128)(2,1)}, u32[]{:S(2)}) %copy-start.8) | copy-done | bytes 131096
  11.1 47.5 %shard_map.214 = (bf16[128,512]{1,0:T(8,128)(2,1)S(1)}, f32[256,512]{1,0:T(8,128)S(1)}, f32[128,512]{1,0:T(8,128)S(1)}, f32[64,256]{1,0:T(8,128)S(1)}, f32[64,25...) custom-call(bf16[256,512]{1,0:T(8,128)(2,1)S(1)} %bitcast.16, ...), custom_call_target="tpu_custom_call" | custom-call | tf_op jit(solution)/shard_map/pallas_call | solution.py:605
  58.7 0.7 %copy.24 = f32[256,64]{0,1:T(8,128)} copy(f32[256,64]{1,0:T(8,128)S(1)} %get-tuple-element.32) | data formatting | bytes 131072
  59.4 0.7 %copy.25 = f32[256,64]{0,1:T(8,128)} copy(f32[256,64]{1,0:T(8,128)S(1)} %get-tuple-element.35) | data formatting | bytes 131072
  60.1 0.7 %copy.35 = bf16[1,128,512]{2,1,0:T(8,128)(2,1)} copy(bf16[1,128,512]{2,1,0:T(8,128)(2,1)S(1)} %bitcast.17) | data formatting | bytes 262144
  60.7 0.8 %copy.36 = f32[1,256,512]{2,1,0:T(8,128)} copy(f32[1,256,512]{2,1,0:T(8,128)S(1)} %bitcast.14) | data formatting | bytes 1048576
  61.5 0.7 %copy.37 = f32[1,128,512]{2,1,0:T(8,128)} copy(f32[1,128,512]{2,1,0:T(8,128)S(1)} %bitcast.15) | data formatting | bytes 524288
  62.2 0.6 copy.38
  62.9 0.6 copy.39
  63.5 0.6 copy.40
  64.1 0.6 copy.41
Async XLA Ops:
  1.9 0.7 %copy-start.12 = (s32[512]{0:T(512)S(1)}, s32[512]{0:T(512)}, u32[]{:S(2)}) copy-start(s32[512]{0:T(512)} %param.28) | copy-start | bytes 6148
  1.9 0.7 %copy-start.11 = (s32[512]{0:T(512)S(1)}, s32[512]{0:T(512)}, u32[]{:S(2)}) copy-start(s32[512]{0:T(512)} %param.27) | copy-start | bytes 6148
  2.0 0.7 %copy-start.10 = (s32[512]{0:T(512)S(1)}, s32[512]{0:T(512)}, u32[]{:S(2)}) copy-start(s32[512]{0:T(512)} %param.25) | copy-start | bytes 6148
  2.0 0.7 %copy-start.9 = (s32[512]{0:T(512)S(1)}, s32[512]{0:T(512)}, u32[]{:S(2)}) copy-start(s32[512]{0:T(512)} %param.24) | copy-start | bytes 6148
  2.7 0.9 %copy-start = (bf16[1,256,512]{2,1,0:T(8,128)(2,1)S(1)}, bf16[1,256,512]{2,1,0:T(8,128)(2,1)}, u32[]{:S(2)}) copy-start(bf16[1,256,512]{2,1,0:T(8,128)(2,1)} %param.15) | copy-start | bytes 786436
  3.6 0.9 %copy-start.1 = (bf16[512,256]{1,0:T(8,128)(2,1)S(1)}, bf16[512,256]{1,0:T(8,128)(2,1)}, u32[]{:S(2)}) copy-start(bf16[512,256]{1,0:T(8,128)(2,1)} %enc_send.1) | copy-start | bytes 786436
  4.6 0.9 %copy-start.2 = (bf16[512,256]{1,0:T(8,128)(2,1)S(1)}, bf16[512,256]{1,0:T(8,128)(2,1)}, u32[]{:S(2)}) copy-start(bf16[512,256]{1,0:T(8,128)(2,1)} %enc_recv.1) | copy-start | bytes 786436
  5.5 0.9 %copy-start.3 = (bf16[256,512]{1,0:T(8,128)(2,1)S(1)}, bf16[256,512]{1,0:T(8,128)(2,1)}, u32[]{:S(2)}) copy-start(bf16[256,512]{1,0:T(8,128)(2,1)} %enc_out.1) | copy-start | bytes 786436
  6.5 0.9 %copy-start.4 = (bf16[512,256]{1,0:T(8,128)(2,1)S(1)}, bf16[512,256]{1,0:T(8,128)(2,1)}, u32[]{:S(2)}) copy-start(bf16[512,256]{1,0:T(8,128)(2,1)} %proc_send.1) | copy-start | bytes 786436
  7.4 0.9 %copy-start.5 = (bf16[512,256]{1,0:T(8,128)(2,1)S(1)}, bf16[512,256]{1,0:T(8,128)(2,1)}, u32[]{:S(2)}) copy-start(bf16[512,256]{1,0:T(8,128)(2,1)} %proc_recv.1) | copy-start | bytes 786436
  8.4 0.9 %copy-start.6 = (bf16[256,512]{1,0:T(8,128)(2,1)S(1)}, bf16[256,512]{1,0:T(8,128)(2,1)}, u32[]{:S(2)}) copy-start(bf16[256,512]{1,0:T(8,128)(2,1)} %proc_out.1) | copy-start | bytes 786436
  9.3 0.9 %copy-start.7 = (bf16[1,128,512]{2,1,0:T(8,128)(2,1)S(1)}, bf16[1,128,512]{2,1,0:T(8,128)(2,1)}, u32[]{:S(2)}) copy-start(bf16[1,128,512]{2,1,0:T(8,128)(2,1)} %param.16) | copy-start | bytes 393220
  10.2 0.9 %copy-start.8 = (bf16[1,128,512]{2,1,0:T(8,128)(2,1)S(1)}, bf16[1,128,512]{2,1,0:T(8,128)(2,1)}, u32[]{:S(2)}) copy-start(bf16[1,128,512]{2,1,0:T(8,128)(2,1)} %param.17) | copy-start | bytes 393220

commit v2 on v1

--- a/solution.py
+++ b/solution.py
@@ -239,49 +239,60 @@
     regions,
     samples,
     cores,
-    grid_ref,
-    mesh_ref,
-    cot_ref,
-    enc_send,
-    enc_recv,
-    enc_out,
-    proc_send,
-    proc_recv,
-    proc_out,
-    enc_sender,
-    enc_receiver,
-    enc_count,
-    proc_sender,
-    proc_receiver,
-    proc_count,
-    mesh_out,
-    grid_grad,
-    mesh_grad,
-    g_enc_send,
-    g_enc_recv,
-    g_enc_out,
-    g_proc_send,
-    g_proc_recv,
-    g_proc_out,
-    req_out,
-    req_in,
-    row_out,
-    row_in,
-    term_out,
-    term_in,
-    part_out,
-    part_in,
-    last_out,
-    last_in,
-    full_grad,
-    pair_out,
-    pair_in,
-    ring_own,
-    ring_out,
-    ring_in,
-    send_sem,
-    recv_sem,
+    *refs,
 ):
+    given, refs = refs[:15], refs[15:]
+    results, refs = refs[:9], refs[9:]
+    held, refs = refs[:15], refs[15:]
+    (
+        grid_ref,
+        mesh_ref,
+        cot_ref,
+        enc_send,
+        enc_recv,
+        enc_out,
+        proc_send,
+        proc_recv,
+        proc_out,
+        enc_sender,
+        enc_receiver,
+        enc_count,
+        proc_sender,
+        proc_receiver,
+        proc_count,
+    ) = held
+    (
+        mesh_out,
+        grid_grad,
+        mesh_grad,
+        g_enc_send,
+        g_enc_recv,
+        g_enc_out,
+        g_proc_send,
+        g_proc_recv,
+        g_proc_out,
+    ) = results
+    (
+        req_out,
+        req_in,
+        row_out,
+        row_in,
+        term_out,
+        term_in,
+        part_out,
+        part_in,
+        last_out,
+        last_in,
+        full_grad,
+        pair_out,
+        pair_in,
+        ring_own,
+        ring_out,
+        ring_in,
+        send_sem,
+        recv_sem,
+        load_sem,
+    ) = refs
     own = lax.axis_index("space")
     sample = lax.axis_index("dp")
     core = lax.axis_index("chan")
@@ -326,12 +337,19 @@
                 friends.append(place(space_at(s_step), sample, core_at(c_step)))
     for d_step in range(1, samples):
         friends.append(place(own, lax.rem(sample + d_step, samples), core))
+    loads = [
+        pltpu.make_async_copy(given[i], held[i], load_sem.at[i]) for i in range(len(given))
+    ]
+    for i in (9, 10, 11, 12, 13, 14, 0, 3, 1, 4, 2, 8, 5, 6, 7):
+        loads[i].start()
     barrier = pltpu.get_barrier_semaphore()
     for friend in friends:
         pl.semaphore_signal(
             barrier, inc=1, device_id=friend, device_id_type=pl.DeviceIdType.MESH
         )
 
+    for i in range(9, 15):
+        loads[i].wait()
     owner_rows = 16
     before = onehot(iota((edges, edges), 0) < iota((edges, edges), 1))
     owner_id = iota((owner_rows, edges), 0)
@@ -397,6 +415,8 @@
     p_pick, p_far, p_recv, p_live, p_pick_t, p_recv_t, p_live_t = tables(
         proc_rows, 4, mesh_total
     )
+    for i in range(9):
+        loads[i].wait()
     grid_block = grid_ref[...]
     mesh_block = mesh_ref[...]
     cot_block = cot_ref[...]
@@ -452,8 +472,7 @@
     proc_gate = jax.nn.sigmoid(proc_pre)
     proc_dpre = (proc_hidden * (proc_gate * (1.0 + proc_pre * (1.0 - proc_gate)))).astype(BF16)
 
-    def send_terms(graph, match, dpre, weights):
-        far = dot(match, dpre).astype(BF16)
+    def send_terms(graph, far, weights):
         term_out[graph] = times_transposed(far, weights).astype(BF16).reshape(regions, CAP, -1)
         copies = []
         for step in range(1, regions):
@@ -465,7 +484,7 @@
                         place(space_at(step), sample, core_at(c_step)),
                     )
                 )
-        return far, copies
+        return copies
 
     def returned(graph, asked):
         return left_transposed(
@@ -473,7 +492,8 @@
             term_in[graph].reshape(cores * slots, -1),
         )
 
-    proc_far, terms = send_terms(1, proc_match, proc_dpre, proc_send[...])
+    proc_far = dot(proc_match, proc_dpre).astype(BF16)
+    terms = send_terms(1, proc_far, proc_send[...])
     everything += terms
     proc_by_sender = dot(p_pick_t, proc_dpre)
     proc_by_receiver = dot(p_recv_t, proc_dpre)
@@ -537,9 +557,8 @@
     shared[4] = share(4, left_transposed(mesh_mid, proc_by_receiver.astype(BF16)))
     part_out[2] = split_dot(proc_act_sum, proc_out[...])
     out_swap = send(part_out.at[2], part_in.at[2], other)
-    for index in (5, 3, 4):
-        everything += shared[index]
     everything.append(out_swap)
+    passed = {}
 
     arrive(terms)
     swapped.wait_recv()
@@ -548,32 +567,34 @@
     )
 
     mid_rounded = mesh_mid_grad.astype(BF16)
+    passed[5] = pass_on(5, shared[5])
     enc_hidden = dot_split(e_live, times_transposed(mid_rounded, enc_out[...]))
     enc_dpre = (enc_hidden * enc_slope).astype(BF16)
     shared[2] = share(2, left_transposed(mid_rounded, enc_act_sum.astype(BF16)))
     enc_by_sender = dot(e_pick_t, enc_dpre)
     enc_by_receiver = dot(e_recv_t, enc_dpre)
-    enc_far, terms = send_terms(0, enc_match, enc_dpre, enc_send[...])
+    enc_far = dot(enc_match, enc_dpre).astype(BF16)
+    passed[3] = pass_on(3, shared[3])
     shared[0] = share(
         0,
         left_transposed(grid_block, enc_by_sender.astype(BF16))
         + left_transposed(far_rows(0), enc_far),
     )
     shared[1] = share(1, left_transposed(mesh_block, enc_by_receiver.astype(BF16)))
+    passed[4] = pass_on(4, shared[4])
+    terms = send_terms(0, enc_far, enc_send[...])
+    everything += terms
     last_out[0:grid_total] = split_dot_transposed(enc_by_sender, enc_send[...])
     last_out[grid_total : grid_total + mesh_total] = split_dot_transposed(
         enc_by_receiver, enc_recv[...]
     )
     last_swap = send(last_out, last_in, other)
-    everything += terms
+    everything.append(last_swap)
+
     for index in (2, 0, 1):
-        everything += shared[index]
-    everything.append(last_swap)
-
-    passed = {}
-    for index in (5, 3, 4, 2, 0, 1):
         passed[index] = pass_on(index, shared[index])
-        everything += passed[index]
+    for index in shared:
+        everything += shared[index] + passed[index]
 
     out_swap.wait_recv()
     mesh_out[...] = (mesh_mid.astype(F32) + (part_out[2] + part_in[2])).astype(BF16)
@@ -583,18 +604,31 @@
     tail = slice(grid_total, grid_total + mesh_total)
     mesh_grad[...] = mesh_mid_grad + (last_out[tail] + last_in[tail])
 
-    g_proc_out[...] = jnp.transpose(finish(5, passed[5]))
+    g_proc_out[...] = finish(5, passed[5])
     g_proc_send[...] = finish(3, passed[3])
     g_proc_recv[...] = finish(4, passed[4])
-    g_enc_out[...] = jnp.transpose(finish(2, passed[2]))
+    g_enc_out[...] = finish(2, passed[2])
     g_enc_send[...] = finish(0, passed[0])
     g_enc_recv[...] = finish(1, passed[1])
     for copy in everything:
         copy.wait_send()
 
 
+def place_kernel(*refs):
+    sources, targets, sems = refs[:9], refs[9:18], refs[18]
+    copies = [
+        pltpu.make_async_copy(sources[i], targets[i], sems.at[i]) for i in range(9)
+    ]
+    for copy in copies:
+        copy.start()
+    for copy in copies:
+        copy.wait()
+
+
 def fused_body(regions, samples, cores, grid, mesh_nodes, cot, *rest):
-    weights, indices = rest[:6], rest[6:]
+    weights = rest[:6]
+    given = [grid[0], mesh_nodes[0], cot[0], *weights]
+    given += [index.reshape(1, -1) for index in rest[6:]]
     grid_total, width = grid.shape[1:]
     mesh_total = mesh_nodes.shape[1]
     hidden = weights[0].shape[1]
@@ -610,14 +644,15 @@
             jax.ShapeDtypeStruct((mesh_total, width), F32),
             jax.ShapeDtypeStruct((shard, hidden), F32),
             jax.ShapeDtypeStruct((shard, hidden), F32),
-            jax.ShapeDtypeStruct((hidden, shard), F32),
             jax.ShapeDtypeStruct((shard, hidden), F32),
             jax.ShapeDtypeStruct((shard, hidden), F32),
-            jax.ShapeDtypeStruct((hidden, shard), F32),
+            jax.ShapeDtypeStruct((shard, hidden), F32),
+            jax.ShapeDtypeStruct((shard, hidden), F32),
         ),
-        in_specs=[vmem] * 15,
+        in_specs=[pl.BlockSpec(memory_space=pl.ANY)] * 15,
         out_specs=(vmem,) * 9,
-        scratch_shapes=[
+        scratch_shapes=[pltpu.VMEM(array.shape, array.dtype) for array in given]
+        + [
             pltpu.VMEM((regions, 2 * CAP, 128), F32),
             pltpu.VMEM((regions, 2 * CAP, 128), F32),
             pltpu.VMEM((2, regions, CAP, width), BF16),
@@ -636,18 +671,21 @@
             pltpu.VMEM((6, regions - 1, shard, hidden), BF16),
             pltpu.SemaphoreType.DMA((copies,)),
             pltpu.SemaphoreType.DMA((copies,)),
+            pltpu.SemaphoreType.DMA((15,)),
         ],
         compiler_params=pltpu.CompilerParams(
-            collective_id=0, has_side_effects=True, vmem_limit_bytes=48 * 2**20
+            collective_id=0, has_side_effects=True, vmem_limit_bytes=58 * 2**20
         ),
-    )(
-        grid[0],
-        mesh_nodes[0],
-        cot[0],
-        *weights,
-        *[index.reshape(1, -1) for index in indices],
-    )
-    return (outs[0][None], outs[1][None], outs[2][None], *outs[3:])
+    )(*given)
+    outs = pl.pallas_call(
+        place_kernel,
+        out_shape=[jax.ShapeDtypeStruct(out.shape, out.dtype) for out in outs],
+        in_specs=[vmem] * 9,
+        out_specs=[pl.BlockSpec(memory_space=pl.ANY)] * 9,
+        scratch_shapes=[pltpu.SemaphoreType.DMA((9,))],
+    )(*outs)
+    gradients = [out.T if i in (2, 5) else out for i, out in enumerate(outs[3:])]
+    return (outs[0][None], outs[1][None], outs[2][None], *gradients)
 
 
 def chosen_body(mesh):

time: 65.2 us -> 54.2 us (0.83)
  local copies, waits for them, and re-layouts: 15.2 us -> 0 us
  Pallas kernels: 47.5 us -> 52.1 us
    unnamed x35 -> x0, local copies, waits for them, and re-layouts: 15.2 us -> none
    pallas_call x0 -> x1, Pallas kernels: none -> 2.37 us  [fused_body(): pl.pallas_call(place_kernel, out_shape=[jax.ShapeDtypeStruct(out.shape, o...]
    pallas_call x1, Pallas kernels: 47.5 us -> 49.7 us  [fused_body(): pl.pallas_call(functools.partial(fused_kernel, regions, samples, cores),...]
where the time goes in v2:
time: 54.2 us; the launch traced here: 54 us
  Pallas kernels  52.1 us (96%)
  between operations  1.95 us (4%)
    pallas_call x1, Pallas kernels, fused_body(): pl.pallas_call(functools.partial(fused_kernel, regions, samples, cores),...  49.7 us
    pallas_call x1, Pallas kernels, fused_body(): pl.pallas_call(place_kernel, out_shape=[jax.ShapeDtypeStruct(out.shape, o...  2.37 us

profile of v2, /device:TPU:0, one launch (start us, length us, event | category | flops | bytes accessed | tf_op | source)
XLA Modules:
  0.0 54.0 jit_solution(8114333049303419334)
XLA Ops:
  1.9 49.7 %shard_map.214 = (bf16[128,512]{1,0:T(8,128)(2,1)}, f32[256,512]{1,0:T(8,128)}, f32[128,512]{1,0:T(8,128)}, f32[64,256]{1,0:T(8,128)}, f32[64,256]{1,0:T(8,128)}...) custom-call(bf16[256,512]{1,0:T(8,128)(2,1)} %bitcast.16, ...), custom_call_target="tpu_custom_call" | custom-call | tf_op jit(solution)/shard_map/pallas_call | solution.py:639
  51.7 2.4 %shard_map.215 = (bf16[128,512]{1,0:T(8,128)(2,1)}, f32[256,512]{1,0:T(8,128)}, f32[128,512]{1,0:T(8,128)}, f32[64,256]{1,0:T(8,128)}, f32[64,256]{1,0:T(8,128)}...) custom-call(bf16[128,512]{1,0:T(8,128)(2,1)} %get-tuple-element.27.refs_0_, ...), custom_call_target="tpu_custom_call" | custom-call | tf_op jit(solution)/shard_map/pallas_call | solution.py:680

commit v3 on v2

--- a/solution.py
+++ b/solution.py
@@ -292,6 +292,10 @@
         send_sem,
         recv_sem,
         load_sem,
+        mid_out,
+        left_in,
+        factor_out,
+        factor_in,
     ) = refs
     own = lax.axis_index("space")
     sample = lax.axis_index("dp")
@@ -420,6 +424,16 @@
     grid_block = grid_ref[...]
     mesh_block = mesh_ref[...]
     cot_block = cot_ref[...]
+
+    def to_samples(src, dst):
+        return [
+            send(src, dst.at[step - 1], place(own, lax.rem(sample + step, samples), core))
+            for step in range(1, samples)
+        ]
+
+    slot_of = {5: 0, 1: 1, 4: 2}
+    left_of = {5: cot_ref, 1: mesh_ref, 4: mid_out}
+    lefts = {5: to_samples(cot_ref, left_in.at[0]), 1: to_samples(mesh_ref, left_in.at[1])}
     enc_pre = dot_split(e_pick, dot(grid_block, enc_send[...])) + dot_split(
         e_recv, dot(mesh_block, enc_recv[...])
     )
@@ -461,47 +475,6 @@
     enc_slope = enc_gate * (1.0 + enc_pre * (1.0 - enc_gate))
     swapped.wait_recv()
     mesh_mid = (mesh_block.astype(F32) + (part_out[0] + part_in[0])).astype(BF16)
-
-    rows_sent = send_rows(1, proc_asked, mesh_mid)
-    everything += rows_sent
-    proc_pre = dot_split(p_pick, dot(mesh_mid, proc_send[...])) + dot_split(
-        p_recv, dot(mesh_mid, proc_recv[...])
-    )
-    arrive(rows_sent)
-    proc_pre = proc_pre + dot_split(p_far, dot(far_rows(1), proc_send[...]))
-    proc_gate = jax.nn.sigmoid(proc_pre)
-    proc_dpre = (proc_hidden * (proc_gate * (1.0 + proc_pre * (1.0 - proc_gate)))).astype(BF16)
-
-    def send_terms(graph, far, weights):
-        term_out[graph] = times_transposed(far, weights).astype(BF16).reshape(regions, CAP, -1)
-        copies = []
-        for step in range(1, regions):
-            for c_step in range(cores):
-                copies.append(
-                    send(
-                        term_out.at[graph, space_at(step)],
-                        term_in.at[graph, core, own],
-                        place(space_at(step), sample, core_at(c_step)),
-                    )
-                )
-        return copies
-
-    def returned(graph, asked):
-        return left_transposed(
-            jnp.concatenate([asked] * cores, axis=0),
-            term_in[graph].reshape(cores * slots, -1),
-        )
-
-    proc_far = dot(proc_match, proc_dpre).astype(BF16)
-    terms = send_terms(1, proc_far, proc_send[...])
-    everything += terms
-    proc_by_sender = dot(p_pick_t, proc_dpre)
-    proc_by_receiver = dot(p_recv_t, proc_dpre)
-    part_out[1] = split_dot_transposed(proc_by_receiver, proc_recv[...]) + split_dot_transposed(
-        proc_by_sender, proc_send[...]
-    )
-    swapped = send(part_out.at[1], part_in.at[1], other)
-    everything.append(swapped)
 
     shard = full_grad.shape[3]
 
@@ -523,11 +496,30 @@
             )
         return copies
 
+    def share_factor(index, factor):
+        slot = slot_of[index]
+        factor_out[slot] = factor.astype(BF16)
+        return to_samples(factor_out.at[slot], factor_in.at[slot])
+
     def pass_on(index, copies):
         arrive(copies)
-        total = full_grad[index, sample]
-        for step in range(1, samples):
-            total = total + pair_in[index, step - 1].astype(F32)
+        if index in slot_of:
+            slot = slot_of[index]
+            arrive(lefts[index])
+            gradient = left_transposed(left_of[index][...], factor_out[slot])
+            for step in range(1, samples):
+                gradient = gradient + left_transposed(
+                    left_in[slot, step - 1], factor_in[slot, step - 1]
+                )
+            for s in range(regions):
+                for d in range(samples):
+                    first = (s * samples + d) * shard
+                    full_grad[index, d, s] = gradient[first : first + shard]
+            total = full_grad[index, sample]
+        else:
+            total = full_grad[index, sample]
+            for step in range(1, samples):
+                total = total + pair_in[index, step - 1].astype(F32)
         ring_own[index] = total
         ring_out[index] = total.astype(BF16)
         return [
@@ -546,19 +538,65 @@
             total = total + ring_in[index, step - 1].astype(F32)
         return total
 
+    rows_sent = send_rows(1, proc_asked, mesh_mid)
+    everything += rows_sent
+    mid_out[...] = mesh_mid
+    lefts[4] = to_samples(mid_out, left_in.at[2])
+    for index in lefts:
+        everything += lefts[index]
+    proc_pre = dot_split(p_pick, dot(mesh_mid, proc_send[...])) + dot_split(
+        p_recv, dot(mesh_mid, proc_recv[...])
+    )
+    arrive(rows_sent)
+    proc_pre = proc_pre + dot_split(p_far, dot(far_rows(1), proc_send[...]))
+    proc_gate = jax.nn.sigmoid(proc_pre)
     proc_act_sum = dot(p_live_t, (proc_pre * proc_gate).astype(BF16))
     shared = {}
-    shared[5] = share(5, left_transposed(cot_block, proc_act_sum.astype(BF16)))
+    shared[5] = share_factor(5, proc_act_sum)
+    proc_dpre = (proc_hidden * (proc_gate * (1.0 + proc_pre * (1.0 - proc_gate)))).astype(BF16)
+
+    def send_terms(graph, far, weights):
+        term_out[graph] = times_transposed(far, weights).astype(BF16).reshape(regions, CAP, -1)
+        copies = []
+        for step in range(1, regions):
+            for c_step in range(cores):
+                copies.append(
+                    send(
+                        term_out.at[graph, space_at(step)],
+                        term_in.at[graph, core, own],
+                        place(space_at(step), sample, core_at(c_step)),
+                    )
+                )
+        return copies
+
+    def returned(graph, asked):
+        return left_transposed(
+            jnp.concatenate([asked] * cores, axis=0),
+            term_in[graph].reshape(cores * slots, -1),
+        )
+
+    proc_far = dot(proc_match, proc_dpre).astype(BF16)
+    terms = send_terms(1, proc_far, proc_send[...])
+    everything += terms
+    proc_by_sender = dot(p_pick_t, proc_dpre)
+    proc_by_receiver = dot(p_recv_t, proc_dpre)
+    part_out[1] = split_dot_transposed(proc_by_receiver, proc_recv[...]) + split_dot_transposed(
+        proc_by_sender, proc_send[...]
+    )
+    swapped = send(part_out.at[1], part_in.at[1], other)
+    everything.append(swapped)
+
     shared[3] = share(
         3,
         left_transposed(mesh_mid, proc_by_sender.astype(BF16))
         + left_transposed(far_rows(1), proc_far),
     )
-    shared[4] = share(4, left_transposed(mesh_mid, proc_by_receiver.astype(BF16)))
+    shared[4] = share_factor(4, proc_by_receiver)
     part_out[2] = split_dot(proc_act_sum, proc_out[...])
     out_swap = send(part_out.at[2], part_in.at[2], other)
     everything.append(out_swap)
     passed = {}
+    passed[5] = pass_on(5, shared[5])
 
     arrive(terms)
     swapped.wait_recv()
@@ -567,21 +605,21 @@
     )
 
     mid_rounded = mesh_mid_grad.astype(BF16)
-    passed[5] = pass_on(5, shared[5])
     enc_hidden = dot_split(e_live, times_transposed(mid_rounded, enc_out[...]))
     enc_dpre = (enc_hidden * enc_slope).astype(BF16)
+    passed[3] = pass_on(3, shared[3])
     shared[2] = share(2, left_transposed(mid_rounded, enc_act_sum.astype(BF16)))
     enc_by_sender = dot(e_pick_t, enc_dpre)
     enc_by_receiver = dot(e_recv_t, enc_dpre)
     enc_far = dot(enc_match, enc_dpre).astype(BF16)
-    passed[3] = pass_on(3, shared[3])
     shared[0] = share(
         0,
         left_transposed(grid_block, enc_by_sender.astype(BF16))
         + left_transposed(far_rows(0), enc_far),
     )
-    shared[1] = share(1, left_transposed(mesh_block, enc_by_receiver.astype(BF16)))
     passed[4] = pass_on(4, shared[4])
+    shared[1] = share_factor(1, enc_by_receiver)
+    passed[2] = pass_on(2, shared[2])
     terms = send_terms(0, enc_far, enc_send[...])
     everything += terms
     last_out[0:grid_total] = split_dot_transposed(enc_by_sender, enc_send[...])
@@ -591,7 +629,7 @@
     last_swap = send(last_out, last_in, other)
     everything.append(last_swap)
 
-    for index in (2, 0, 1):
+    for index in (0, 1):
         passed[index] = pass_on(index, shared[index])
     for index in shared:
         everything += shared[index] + passed[index]
@@ -634,7 +672,7 @@
     hidden = weights[0].shape[1]
     shard = width // (regions * samples)
     last_total = grid_total + mesh_total
-    copies = (regions - 1) * (3 + 2 * cores + 6) + 6 * (samples - 1) + 4
+    copies = (regions - 1) * (3 + 2 * cores + 6) + 9 * (samples - 1) + 4
     vmem = pl.BlockSpec(memory_space=pltpu.VMEM)
     outs = pl.pallas_call(
         functools.partial(fused_kernel, regions, samples, cores),
@@ -672,6 +710,10 @@
             pltpu.SemaphoreType.DMA((copies,)),
             pltpu.SemaphoreType.DMA((copies,)),
             pltpu.SemaphoreType.DMA((15,)),
+            pltpu.VMEM((mesh_total, width), BF16),
+            pltpu.VMEM((3, samples - 1, mesh_total, width), BF16),
+            pltpu.VMEM((3, mesh_total, hidden), BF16),
+            pltpu.VMEM((3, samples - 1, mesh_total, hidden), BF16),
         ],
         compiler_params=pltpu.CompilerParams(
             collective_id=0, has_side_effects=True, vmem_limit_bytes=58 * 2**20

time: 54.2 us -> 52.2 us (0.963)
  Pallas kernels: 52.1 us -> 50 us
    pallas_call x1, Pallas kernels: 49.7 us -> 47.7 us  [fused_body(): pl.pallas_call(functools.partial(fused_kernel, regions, samples, cores),...]
where the time goes in v3:
time: 52.2 us; the launch traced here: 52 us
  Pallas kernels  50 us (96%)
  between operations  1.95 us (4%)
    pallas_call x1, Pallas kernels, fused_body(): pl.pallas_call(functools.partial(fused_kernel, regions, samples, cores),...  47.7 us
    pallas_call x1, Pallas kernels, fused_body(): pl.pallas_call(place_kernel, out_shape=[jax.ShapeDtypeStruct(out.shape, o...  2.37 us

profile of v3, /device:TPU:0, one launch (start us, length us, event | category | flops | bytes accessed | tf_op | source)
XLA Modules:
  0.0 52.0 jit_solution(3501022172096178304)
XLA Ops:
  1.9 47.7 %shard_map.214 = (bf16[128,512]{1,0:T(8,128)(2,1)}, f32[256,512]{1,0:T(8,128)}, f32[128,512]{1,0:T(8,128)}, f32[64,256]{1,0:T(8,128)}, f32[64,256]{1,0:T(8,128)}...) custom-call(bf16[256,512]{1,0:T(8,128)(2,1)} %bitcast.16, ...), custom_call_target="tpu_custom_call" | custom-call | tf_op jit(solution)/shard_map/pallas_call | solution.py:677
  49.6 2.4 %shard_map.215 = (bf16[128,512]{1,0:T(8,128)(2,1)}, f32[256,512]{1,0:T(8,128)}, f32[128,512]{1,0:T(8,128)}, f32[64,256]{1,0:T(8,128)}, f32[64,256]{1,0:T(8,128)}...) custom-call(bf16[128,512]{1,0:T(8,128)(2,1)} %get-tuple-element.27.refs_0_, ...), custom_call_target="tpu_custom_call" | custom-call | tf_op jit(solution)/shard_map/pallas_call | solution.py:722
